TPU v7x, 128 devices: a whole 4x4x4 slice. The times are simulated.
128 devices in a mesh: leaf: 4 (over y), dp: 32 (over z, x, core).
Axes of the slice: x: 4, y: 4, z: 4, core: 2. Of those that a mesh axis runs over, the one named last changes fastest.
Arguments:
- bins: int32 [49152, 256], P('dp'), may hold values from 0 to 255
- outcome: float32 [49152], P('dp'), may hold values from -6 to 6
- treatment: int32 [49152], P('dp'), may hold values 0 or 1
- bag: int32 [196608], P(('leaf', 'dp')), parts along dimension 0, may hold values 0 or 1
- block_node: int32 [384], P('dp'), may hold values from 0 to 15, as said below
Outputs:
- hist_sum: float32 [1024, 16, 256], P(('leaf', 'dp')), parts along dimension 0
- hist_count: float32 [1024, 16, 256], P(('leaf', 'dp')), parts along dimension 0
There are 4 independent parts, one for each index of `leaf`. A program takes and returns all parts, laid end to end along the dimension named above; an argument that names none is the same for every part. Nothing has to cross between parts.
Inputs may be any that keep to these rules, and one draw needn't show every extreme that they name: block_node is nondecreasing along the blocks; every node has 1 to 128 blocks, one exactly that many.
All inputs are finite; a program needn't handle non-finite values. No bound on the sum of `treatment` or of `bag` on one device may be relied on, other than what follows from the above.
Results may differ from a plain program's by a relative error of at most 0.0029.
Values may be sent and summed in bfloat16 or wider, within the bound.
No kernel may reach another device: no remote copies, remote signals or barrier semaphores. Data moves between devices by JAX's collectives and lax.ppermute only.
A program may use at most 64 MiB of HBM per device.

v0:
```python
import math

import jax
import jax.numpy as jnp
from jax import lax
from jax.sharding import PartitionSpec as P

BINS = 256
NODES = 16


def node_params(moments):
    count_n = moments[:, 0]
    sum_w = moments[:, 1]
    sum_y = moments[:, 2]
    sum_wy = moments[:, 3]
    shrunk = count_n + 1.0
    wbar = sum_w / shrunk
    ybar = sum_y / shrunk
    cov = sum_wy - wbar * sum_y - ybar * sum_w + count_n * wbar * ybar
    spread = sum_w - 2.0 * wbar * sum_w + count_n * wbar * wbar + 1.0
    effect = cov / spread
    return jnp.stack([wbar, ybar, effect, shrunk / spread], 1)


def histogram_term(bins, left, count):
    row_count = bins.shape[0]
    width = left.shape[1]
    group = math.gcd(count, 16)
    grouped = bins.reshape(row_count, count // group, group).transpose(1, 0, 2)

    def one_group(picked):
        table = (picked[:, :, None] == jnp.arange(BINS, dtype=jnp.int32)[None, None, :]).astype(
            jnp.bfloat16
        )
        return jnp.einsum("rm,rgb->gmb", left, table, preferred_element_type=jnp.float32)

    return lax.map(one_group, grouped).reshape(count, width, BINS)


def shards(bins, outcome, treatment, bag, block_node):
    row_count = bins.shape[0]
    block_count = block_node.shape[0]
    per_block = row_count // block_count
    own_features = bins.shape[1] // lax.axis_size("dp")
    block_hot = (block_node[:, None] == jnp.arange(NODES, dtype=jnp.int32)[None, :]).astype(
        jnp.float32
    )
    weight = treatment.astype(jnp.float32)
    taken = bag.astype(jnp.float32)
    taken_low = taken.astype(jnp.bfloat16)
    stats = jnp.stack([taken, taken * weight, taken * outcome, taken * weight * outcome], 1)
    block_stats = stats.reshape(block_count, per_block, 4).sum(axis=1)
    local_moments = jnp.dot(block_hot.T, block_stats, precision=lax.Precision.HIGHEST)
    row_hot = jnp.repeat(block_hot, per_block, axis=0).astype(jnp.bfloat16)
    count_left = row_hot * taken_low[:, None]
    moments = lax.psum(local_moments, "dp")
    params = node_params(moments)
    block_params = jnp.dot(block_hot, params, precision=lax.Precision.HIGHEST)
    row_params = jnp.repeat(block_params, per_block, axis=0)
    centred = weight - row_params[:, 0]
    rho = (
        taken
        * centred
        * (outcome - row_params[:, 1] - centred * row_params[:, 2])
        * row_params[:, 3]
    )
    rho_low = rho.astype(jnp.bfloat16)
    sum_left = row_hot * rho_low[:, None]
    both_left = jnp.concatenate([sum_left, count_left], axis=1)
    both = lax.psum_scatter(
        histogram_term(bins, both_left, own_features * lax.axis_size("dp")),
        "dp",
        scatter_dimension=0,
        tiled=True,
    )
    hist_sum = both[:, :NODES]
    hist_count = both[:, NODES:]
    return (hist_sum, hist_count)


def solution(mesh):
    return jax.shard_map(
        shards,
        mesh=mesh,
        in_specs=(P("dp", None), P("dp"), P("dp"), P(("leaf", "dp")), P("dp")),
        out_specs=(P(("leaf", "dp"), None, None), P(("leaf", "dp"), None, None)),
        check_vma=False,
    )
```

profile of v0, /device:TPU:1, one launch (start us, length us, event | category | flops | bytes accessed | tf_op | source)
XLA Modules:
  0.0 304.7 jit_solution(4352091207590178504)
XLA Ops:
  7.2 0.0 reduce-scatter.2.cloned.1.call-start
  7.2 0.7 convert_bitcast_fusion
  7.9 0.7 convert_convert_fusion.1
  8.6 0.7 fusion.9
  9.3 0.1 maximum_reduce_fusion
  9.4 0.8 fusion.6
  10.2 64.8 %psum.7 = f32[16,4]{0,1:T(4,128)S(1)} all-reduce(f32[16,4]{0,1:T(4,128)S(1)} %fusion.6), channel_id=1, replica_groups=mesh['leaf'=4,'dp'=32] {'dp'}, use_global_device_ids=true, to_apply=%region_1.0 | all-reduce | flops 64 | bytes 512 | tf_op jit(solution)/shard_map/psum | solution.py:57
  75.0 0.8 fusion.5
  75.8 0.1 broadcast_bitcast_fusion
  75.9 0.1 slice_reduce_fusion.3
  76.0 1.9 copy.11
  77.9 0.7 multiply_convert_fusion
  78.6 0.1 broadcast_in_dim.20
  78.8 125.3 %while.10 = (s32[]{:T(128)}, f32[16,16,32,256]{3,2,1,0:T(8,128)}, s32[16,1536,16]{1,2,0:T(8,128)S(1)}, bf16[1536,32]{0,1:T(8,128)(2,1)S(1)}, s32[]{:T(128)}) while((s32[]{:T(128)}, f32[16,16,32,256]{3,2,1,0:T(8,128)}, s32[16,1536,16]{1,2,0:T(8,128)S(1)}, bf16[1536,32]{0,1:T(8,128)(2,1)S(1)}, s32[]{:T(128)}) %tuple.37), condition=%wide.region_3.4_spmd, body=%wide.region_2.3_spmd.sunk | while | flops 408944640 | bytes 918081 | solution.py:38
  78.8 7.8 %fusion.28 = f32[16,16,32,256]{3,2,1,0:T(8,128)} fusion(f32[16,16,32,256]{3,2,1,0:T(8,128)} %get-tuple-element.80, s32[]{:T(128)} %get-tuple-element.79, s32[1536,16]{0,1:T(8,128)S(1)} %dynamic-slice_bitcast_fusion.2, bf16[1536,32]{0,1:T(8,128)(2,1)S(1)} %get-tuple-element.87), kind=kOutput, calls=%fused_computation.4.clone.1 | convolution fusion | flops 408944640 | bytes 721408 | tf_op jit(solution)/shard_map/while/body/eval_jaxpr/rm,rgb->gmb/dot_general | solution.py:36
  86.6 7.8 %fusion.28 = f32[16,16,32,256]{3,2,1,0:T(8,128)} fusion(f32[16,16,32,256]{3,2,1,0:T(8,128)} %get-tuple-element.80, s32[]{:T(128)} %get-tuple-element.79, s32[1536,16]{0,1:T(8,128)S(1)} %dynamic-slice_bitcast_fusion.2, bf16[1536,32]{0,1:T(8,128)(2,1)S(1)} %get-tuple-element.87), kind=kOutput, calls=%fused_computation.4.clone.1 | convolution fusion | flops 408944640 | bytes 721408 | tf_op jit(solution)/shard_map/while/body/eval_jaxpr/rm,rgb->gmb/dot_general | solution.py:36
  94.5 7.8 %fusion.28 = f32[16,16,32,256]{3,2,1,0:T(8,128)} fusion(f32[16,16,32,256]{3,2,1,0:T(8,128)} %get-tuple-element.80, s32[]{:T(128)} %get-tuple-element.79, s32[1536,16]{0,1:T(8,128)S(1)} %dynamic-slice_bitcast_fusion.2, bf16[1536,32]{0,1:T(8,128)(2,1)S(1)} %get-tuple-element.87), kind=kOutput, calls=%fused_computation.4.clone.1 | convolution fusion | flops 408944640 | bytes 721408 | tf_op jit(solution)/shard_map/while/body/eval_jaxpr/rm,rgb->gmb/dot_general | solution.py:36
  102.3 7.8 %fusion.28 = f32[16,16,32,256]{3,2,1,0:T(8,128)} fusion(f32[16,16,32,256]{3,2,1,0:T(8,128)} %get-tuple-element.80, s32[]{:T(128)} %get-tuple-element.79, s32[1536,16]{0,1:T(8,128)S(1)} %dynamic-slice_bitcast_fusion.2, bf16[1536,32]{0,1:T(8,128)(2,1)S(1)} %get-tuple-element.87), kind=kOutput, calls=%fused_computation.4.clone.1 | convolution fusion | flops 408944640 | bytes 721408 | tf_op jit(solution)/shard_map/while/body/eval_jaxpr/rm,rgb->gmb/dot_general | solution.py:36
  110.1 7.8 %fusion.28 = f32[16,16,32,256]{3,2,1,0:T(8,128)} fusion(f32[16,16,32,256]{3,2,1,0:T(8,128)} %get-tuple-element.80, s32[]{:T(128)} %get-tuple-element.79, s32[1536,16]{0,1:T(8,128)S(1)} %dynamic-slice_bitcast_fusion.2, bf16[1536,32]{0,1:T(8,128)(2,1)S(1)} %get-tuple-element.87), kind=kOutput, calls=%fused_computation.4.clone.1 | convolution fusion | flops 408944640 | bytes 721408 | tf_op jit(solution)/shard_map/while/body/eval_jaxpr/rm,rgb->gmb/dot_general | solution.py:36
  118.0 7.8 %fusion.28 = f32[16,16,32,256]{3,2,1,0:T(8,128)} fusion(f32[16,16,32,256]{3,2,1,0:T(8,128)} %get-tuple-element.80, s32[]{:T(128)} %get-tuple-element.79, s32[1536,16]{0,1:T(8,128)S(1)} %dynamic-slice_bitcast_fusion.2, bf16[1536,32]{0,1:T(8,128)(2,1)S(1)} %get-tuple-element.87), kind=kOutput, calls=%fused_computation.4.clone.1 | convolution fusion | flops 408944640 | bytes 721408 | tf_op jit(solution)/shard_map/while/body/eval_jaxpr/rm,rgb->gmb/dot_general | solution.py:36
  125.8 7.8 %fusion.28 = f32[16,16,32,256]{3,2,1,0:T(8,128)} fusion(f32[16,16,32,256]{3,2,1,0:T(8,128)} %get-tuple-element.80, s32[]{:T(128)} %get-tuple-element.79, s32[1536,16]{0,1:T(8,128)S(1)} %dynamic-slice_bitcast_fusion.2, bf16[1536,32]{0,1:T(8,128)(2,1)S(1)} %get-tuple-element.87), kind=kOutput, calls=%fused_computation.4.clone.1 | convolution fusion | flops 408944640 | bytes 721408 | tf_op jit(solution)/shard_map/while/body/eval_jaxpr/rm,rgb->gmb/dot_general | solution.py:36
  133.6 7.8 %fusion.28 = f32[16,16,32,256]{3,2,1,0:T(8,128)} fusion(f32[16,16,32,256]{3,2,1,0:T(8,128)} %get-tuple-element.80, s32[]{:T(128)} %get-tuple-element.79, s32[1536,16]{0,1:T(8,128)S(1)} %dynamic-slice_bitcast_fusion.2, bf16[1536,32]{0,1:T(8,128)(2,1)S(1)} %get-tuple-element.87), kind=kOutput, calls=%fused_computation.4.clone.1 | convolution fusion | flops 408944640 | bytes 721408 | tf_op jit(solution)/shard_map/while/body/eval_jaxpr/rm,rgb->gmb/dot_general | solution.py:36
  141.5 7.8 %fusion.28 = f32[16,16,32,256]{3,2,1,0:T(8,128)} fusion(f32[16,16,32,256]{3,2,1,0:T(8,128)} %get-tuple-element.80, s32[]{:T(128)} %get-tuple-element.79, s32[1536,16]{0,1:T(8,128)S(1)} %dynamic-slice_bitcast_fusion.2, bf16[1536,32]{0,1:T(8,128)(2,1)S(1)} %get-tuple-element.87), kind=kOutput, calls=%fused_computation.4.clone.1 | convolution fusion | flops 408944640 | bytes 721408 | tf_op jit(solution)/shard_map/while/body/eval_jaxpr/rm,rgb->gmb/dot_general | solution.py:36
  149.3 7.8 %fusion.28 = f32[16,16,32,256]{3,2,1,0:T(8,128)} fusion(f32[16,16,32,256]{3,2,1,0:T(8,128)} %get-tuple-element.80, s32[]{:T(128)} %get-tuple-element.79, s32[1536,16]{0,1:T(8,128)S(1)} %dynamic-slice_bitcast_fusion.2, bf16[1536,32]{0,1:T(8,128)(2,1)S(1)} %get-tuple-element.87), kind=kOutput, calls=%fused_computation.4.clone.1 | convolution fusion | flops 408944640 | bytes 721408 | tf_op jit(solution)/shard_map/while/body/eval_jaxpr/rm,rgb->gmb/dot_general | solution.py:36
  157.1 7.8 %fusion.28 = f32[16,16,32,256]{3,2,1,0:T(8,128)} fusion(f32[16,16,32,256]{3,2,1,0:T(8,128)} %get-tuple-element.80, s32[]{:T(128)} %get-tuple-element.79, s32[1536,16]{0,1:T(8,128)S(1)} %dynamic-slice_bitcast_fusion.2, bf16[1536,32]{0,1:T(8,128)(2,1)S(1)} %get-tuple-element.87), kind=kOutput, calls=%fused_computation.4.clone.1 | convolution fusion | flops 408944640 | bytes 721408 | tf_op jit(solution)/shard_map/while/body/eval_jaxpr/rm,rgb->gmb/dot_general | solution.py:36
  164.9 7.8 %fusion.28 = f32[16,16,32,256]{3,2,1,0:T(8,128)} fusion(f32[16,16,32,256]{3,2,1,0:T(8,128)} %get-tuple-element.80, s32[]{:T(128)} %get-tuple-element.79, s32[1536,16]{0,1:T(8,128)S(1)} %dynamic-slice_bitcast_fusion.2, bf16[1536,32]{0,1:T(8,128)(2,1)S(1)} %get-tuple-element.87), kind=kOutput, calls=%fused_computation.4.clone.1 | convolution fusion | flops 408944640 | bytes 721408 | tf_op jit(solution)/shard_map/while/body/eval_jaxpr/rm,rgb->gmb/dot_general | solution.py:36
  172.8 7.8 %fusion.28 = f32[16,16,32,256]{3,2,1,0:T(8,128)} fusion(f32[16,16,32,256]{3,2,1,0:T(8,128)} %get-tuple-element.80, s32[]{:T(128)} %get-tuple-element.79, s32[1536,16]{0,1:T(8,128)S(1)} %dynamic-slice_bitcast_fusion.2, bf16[1536,32]{0,1:T(8,128)(2,1)S(1)} %get-tuple-element.87), kind=kOutput, calls=%fused_computation.4.clone.1 | convolution fusion | flops 408944640 | bytes 721408 | tf_op jit(solution)/shard_map/while/body/eval_jaxpr/rm,rgb->gmb/dot_general | solution.py:36
  180.6 7.8 %fusion.28 = f32[16,16,32,256]{3,2,1,0:T(8,128)} fusion(f32[16,16,32,256]{3,2,1,0:T(8,128)} %get-tuple-element.80, s32[]{:T(128)} %get-tuple-element.79, s32[1536,16]{0,1:T(8,128)S(1)} %dynamic-slice_bitcast_fusion.2, bf16[1536,32]{0,1:T(8,128)(2,1)S(1)} %get-tuple-element.87), kind=kOutput, calls=%fused_computation.4.clone.1 | convolution fusion | flops 408944640 | bytes 721408 | tf_op jit(solution)/shard_map/while/body/eval_jaxpr/rm,rgb->gmb/dot_general | solution.py:36
  188.4 7.8 %fusion.28 = f32[16,16,32,256]{3,2,1,0:T(8,128)} fusion(f32[16,16,32,256]{3,2,1,0:T(8,128)} %get-tuple-element.80, s32[]{:T(128)} %get-tuple-element.79, s32[1536,16]{0,1:T(8,128)S(1)} %dynamic-slice_bitcast_fusion.2, bf16[1536,32]{0,1:T(8,128)(2,1)S(1)} %get-tuple-element.87), kind=kOutput, calls=%fused_computation.4.clone.1 | convolution fusion | flops 408944640 | bytes 721408 | tf_op jit(solution)/shard_map/while/body/eval_jaxpr/rm,rgb->gmb/dot_general | solution.py:36
  196.3 7.8 %fusion.28 = f32[16,16,32,256]{3,2,1,0:T(8,128)} fusion(f32[16,16,32,256]{3,2,1,0:T(8,128)} %get-tuple-element.80, s32[]{:T(128)} %get-tuple-element.79, s32[1536,16]{0,1:T(8,128)S(1)} %dynamic-slice_bitcast_fusion.2, bf16[1536,32]{0,1:T(8,128)(2,1)S(1)} %get-tuple-element.87), kind=kOutput, calls=%fused_computation.4.clone.1 | convolution fusion | flops 408944640 | bytes 721408 | tf_op jit(solution)/shard_map/while/body/eval_jaxpr/rm,rgb->gmb/dot_general | solution.py:36
  204.1 0.0 reduce-scatter.2.cloned.1.call-update
  204.1 92.1 %reduce-scatter.2.cloned.1.call-done = f32[8,32,256]{2,1,0:T(8,128)} async-done(((f32[256,32,256]{2,1,0:T(8,128)}), f32[8,32,256]{2,1,0:T(8,128)}) %reduce-scatter.2.cloned.1.call-update) | async-done | bytes 262160 | tf_op jit(solution)/shard_map/reduce_scatter | solution.py:71
  296.2 1.7 fusion.23
  (22 shorter events, 0.2 us)
Async XLA Ops:
  7.2 289.0 %reduce-scatter.2.cloned.1.call-start = ((), (), s32[]{:S(2)}) async-start(), calls=%async_computation.1 | async-start | bytes 8650752 | tf_op jit(solution)/shard_map/reduce_scatter | solution.py:71
Sparse Core Ops, SparseCore 0:
  204.2 91.9 reduce-scatter.1
where the time goes:
time: 306 us; the launch traced here: 305 us
  matrix products  127 us (42%)
  waiting for transfers between devices  92.1 us (30%)
  blocking collectives  64.8 us (21%)
  between operations  14.1 us (5%)
  local copies, waits for them, and re-layouts  3.94 us (1%)
    dot_general x16, matrix products, one_group(): jnp.einsum('rm,rgb->gmb', left, table, preferred_element_type=jnp.float32)  125 us
    reduce_scatter x1, waiting for transfers between devices, shards(): lax.psum_scatter(histogram_term(bins, both_left, own_features * lax.axis_...  92.1 us
    psum x1, blocking collectives, shards(): moments = lax.psum(local_moments, 'dp')  64.8 us
  transfers between devices with their start and end apart: 1, of which 1 were waited for; matrix products, arithmetic and copies ran while one was open for 0% of the time, Pallas kernels for 0%

commit v1 on v0

v1 whole, which is shorter than its diff:
```python
import functools

import jax
import jax.numpy as jnp
from jax import lax
from jax.experimental import pallas as pl
from jax.experimental.pallas import tpu as pltpu
from jax.sharding import PartitionSpec as P

BINS = 256
NODES = 16
LANES = 128
SLOTS = 16
F32 = jnp.float32
BF16 = jnp.bfloat16
I32 = jnp.int32
I16 = jnp.int16
Y_SCALE = float(2**28)


def pack_kernel(bins_ref, y_ref, w_ref, b_ref, node_ref, out_ref):
    dests = out_ref.shape[0]
    blocks = y_ref.shape[0]
    half = blocks // 2
    for t in range(half):
        low = bins_ref[pl.ds(LANES * t, LANES), :]
        high = bins_ref[pl.ds(LANES * (t + half), LANES), :]
        packed = jnp.bitwise_or(low, lax.shift_left(high, 16)).T
        out_ref[:, pl.ds(8 * t, 8), :] = packed.reshape(dests, 8, LANES)
    base = 8 * half
    fixed = jnp.round(y_ref[...] * Y_SCALE).astype(I32)
    flags = jnp.bitwise_or(w_ref[...], lax.shift_left(b_ref[...], 16))
    tail = jnp.concatenate(
        [
            fixed,
            node_ref[...],
            jnp.zeros((SLOTS - blocks - 1, LANES), I32),
            flags,
            jnp.zeros((SLOTS - blocks, LANES), I32),
        ],
        axis=0,
    )
    out_ref[:, pl.ds(base, 2 * SLOTS), :] = jnp.broadcast_to(tail[None], (dests,) + tail.shape)


def split3(x):
    high = x.astype(BF16)
    rest = x - high.astype(F32)
    mid = rest.astype(BF16)
    low = (rest - mid.astype(F32)).astype(BF16)
    return high, mid, low


def hist_kernel(node_smem, recv_ref, sum_ref, cnt_ref, rho_ref, bag_ref, acc_ref, *, blocks):
    sources = recv_ref.shape[0]
    half = blocks // 2
    base = 8 * half
    rows = sources * SLOTS

    first = recv_ref[:, pl.ds(base, SLOTS), :]
    flags = recv_ref[:, pl.ds(base + SLOTS, SLOTS), :].reshape(rows, LANES)
    y = first.reshape(rows, LANES).astype(F32) * (1.0 / Y_SCALE)
    w = jnp.bitwise_and(flags, 0xFFFF).astype(F32)
    b = lax.shift_right_logical(flags, 16).astype(F32)
    sub = lax.broadcasted_iota(I32, (sources, SLOTS, LANES), 1)
    lane = lax.broadcasted_iota(I32, (sources, SLOTS, LANES), 2)
    node_row = jnp.broadcast_to(first[:, blocks : blocks + 1, :], first.shape).astype(F32)
    node_col = jnp.sum(jnp.where(sub == lane, node_row, 0.0), axis=2, keepdims=True)
    node_col = node_col.reshape(rows, 1)
    lanes = lax.broadcasted_iota(I32, (rows, LANES), 1)
    wanted = jnp.where(lanes < 3 * NODES, jnp.bitwise_and(lanes, NODES - 1), -1).astype(F32)
    hot3 = (jnp.broadcast_to(node_col, (rows, LANES)) == wanted).astype(F32)
    hot_t = hot3.T.astype(BF16)[:NODES]
    bw = b * w
    stats = jnp.concatenate(
        [b.astype(BF16), bw.astype(BF16), *split3(b * y), *split3(bw * y)], axis=1
    )
    sums = jnp.dot(hot_t, stats, preferred_element_type=F32)

    def total(first_part, parts):
        out = sums[:, LANES * first_part : LANES * (first_part + 1)]
        for p in range(1, parts):
            out = out + sums[:, LANES * (first_part + p) : LANES * (first_part + p + 1)]
        return jnp.sum(out, axis=1, keepdims=True)

    count_n = total(0, 1)
    sum_w = total(1, 1)
    sum_y = total(2, 3)
    sum_wy = total(5, 3)
    shrunk = count_n + 1.0
    wbar = sum_w / shrunk
    ybar = sum_y / shrunk
    cov = sum_wy - wbar * sum_y - ybar * sum_w + count_n * wbar * ybar
    spread = sum_w - 2.0 * wbar * sum_w + count_n * wbar * wbar + 1.0
    effect = cov / spread
    scale = shrunk / spread
    params = jnp.concatenate(
        [jnp.broadcast_to(p, (NODES, LANES)) for p in (wbar, ybar, effect, scale)], axis=1
    )
    params = jnp.concatenate(
        [*split3(params), jnp.zeros((LANES - 3 * NODES, 4 * LANES), BF16)], axis=0
    )
    spread_out = jnp.dot(hot3.astype(BF16), params, preferred_element_type=F32)
    r_wbar, r_ybar, r_effect, r_scale = [
        spread_out[:, LANES * p : LANES * (p + 1)] for p in range(4)
    ]
    centred = w - r_wbar
    rho_ref[...] = b * centred * ((y - r_ybar) - centred * r_effect) * r_scale
    bag_ref[...] = b

    acc_ref[...] = jnp.zeros_like(acc_ref)
    iota_hi = jnp.bitwise_and(lax.broadcasted_iota(I32, (16, LANES), 0), 7).astype(I16)
    iota_lo = lax.broadcasted_iota(I32, (32, LANES), 0).astype(I16)
    lane_group = lax.shift_right_logical(lax.broadcasted_iota(I32, (16, LANES), 1), 5)
    one = jnp.ones((32, LANES), BF16)
    zero_lo = jnp.zeros((32, LANES), BF16)
    zero_hi = jnp.zeros((16, LANES), BF16)

    def one_source(s, carry):
        for k in range(blocks):
            tile = recv_ref[s, pl.ds(8 * (k % half), 8), :]
            if k < half:
                tile = jnp.bitwise_and(tile, 0xFFFF)
            else:
                tile = lax.shift_right_logical(tile, 16)
            hi = lax.shift_right_logical(tile, 5)
            lo = jnp.bitwise_and(tile, 31)
            row = s * SLOTS + k
            vals = jnp.concatenate(
                [
                    jnp.broadcast_to(rho_ref[pl.ds(row, 1), :], (8, LANES)),
                    jnp.broadcast_to(bag_ref[pl.ds(row, 1), :], (8, LANES)),
                ],
                axis=0,
            ).astype(BF16)
            node = node_smem[s, k]
            for q in range(2):
                left, right = [], []
                for f in range(4 * q, 4 * q + 4):
                    hi_f = jnp.broadcast_to(hi[f : f + 1], (16, LANES)).astype(I16)
                    lo_f = jnp.broadcast_to(lo[f : f + 1], (32, LANES)).astype(I16)
                    left.append(jnp.where(hi_f == iota_hi, vals, zero_hi))
                    right.append(jnp.where(lo_f == iota_lo, one, zero_lo))
                prod = lax.dot_general(
                    jnp.concatenate(left, axis=0),
                    jnp.concatenate(right, axis=0),
                    (((1,), (1,)), ((), ())),
                    preferred_element_type=F32,
                )
                merged = prod[0:16]
                for i in range(1, 4):
                    merged = jnp.where(lane_group == i, prod[16 * i : 16 * i + 16], merged)
                acc_ref[node, pl.ds(16 * q, 16), :] += merged
        return carry

    lax.fori_loop(0, sources, one_source, 0)

    for v, out_ref in enumerate((sum_ref, cnt_ref)):
        for q in range(2):
            for c in range(2):
                pieces = [acc_ref[:, 16 * q + 8 * v + 4 * c + g, :] for g in range(4)]
                for i in range(4):
                    out = None
                    for g in range(4):
                        shift = (32 * (g - i)) % LANES
                        moved = pltpu.roll(pieces[g], shift, 1) if shift else pieces[g]
                        out = moved if out is None else jnp.where(lane_group == g, moved, out)
                    out_ref[4 * q + i, :, pl.ds(LANES * c, LANES)] = out


def shards(bins, outcome, treatment, bag, block_node):
    blocks = block_node.shape[0]
    dests = lax.axis_size("dp")
    own = bins.shape[1] // dests
    height = 8 * (blocks // 2) + 2 * SLOTS
    node_row = jnp.pad(block_node, (0, LANES - blocks)).reshape(1, LANES)
    packed = pl.pallas_call(
        pack_kernel,
        out_shape=jax.ShapeDtypeStruct((dests, height, LANES), I32),
        compiler_params=pltpu.CompilerParams(vmem_limit_bytes=32 * 2**20),
        name="pack",
    )(
        bins,
        outcome.reshape(blocks, LANES),
        treatment.reshape(blocks, LANES),
        bag.reshape(blocks, LANES),
        node_row,
    )
    recv = lax.all_to_all(packed, "dp", 0, 0, tiled=True)
    nodes = recv[:, 8 * (blocks // 2) + blocks, :blocks]
    out = jax.ShapeDtypeStruct((own, NODES, BINS), F32)
    vmem = pl.BlockSpec(memory_space=pltpu.VMEM)
    return pl.pallas_call(
        functools.partial(hist_kernel, blocks=blocks),
        out_shape=(out, out),
        in_specs=[pl.BlockSpec(memory_space=pltpu.SMEM), vmem],
        out_specs=(vmem, vmem),
        scratch_shapes=[
            pltpu.VMEM((dests * SLOTS, LANES), F32),
            pltpu.VMEM((dests * SLOTS, LANES), F32),
            pltpu.VMEM((NODES, 32, LANES), F32),
        ],
        compiler_params=pltpu.CompilerParams(vmem_limit_bytes=32 * 2**20),
        name="hist",
    )(nodes, recv)


def solution(mesh):
    return jax.shard_map(
        shards,
        mesh=mesh,
        in_specs=(P("dp", None), P("dp"), P("dp"), P(("leaf", "dp")), P("dp")),
        out_specs=(P(("leaf", "dp"), None, None), P(("leaf", "dp"), None, None)),
        check_vma=False,
    )
```

time: 306 us -> 58 us (0.19)
  matrix products: 127 us -> 0 us
  waiting for transfers between devices: 92.1 us -> 0 us
  blocking collectives: 64.8 us -> 29.4 us
  Pallas kernels: 0 us -> 23.5 us
  between operations: 14.1 us -> 0.64 us
    dot_general x18 -> x0, matrix products: 127 us -> none  [the longest x16 125 us: one_group(): jnp.einsum('rm,rgb->gmb', left, table, preferred_element_type=jnp.float32)]
    reduce_scatter x1 -> x0, waiting for transfers between devices: 92.1 us -> none  [shards(): lax.psum_scatter(histogram_term(bins, both_left, own_features * lax.axis_...]
    psum x1 -> x0, blocking collectives: 64.8 us -> none  [shards(): moments = lax.psum(local_moments, 'dp')]
    all_to_all x0 -> x1, blocking collectives: none -> 29.4 us  [shards(): recv = lax.all_to_all(packed, 'dp', 0, 0, tiled=True)]
    pallas_call x0 -> x2, Pallas kernels: none -> 23.5 us  [the longest x1 23.2 us: shards(): pl.pallas_call(functools.partial(hist_kernel, blocks=blocks), out_shape=(...]
  transfers between devices with their start and end apart: 1 -> 0, of which waited for: 1 -> 0; matrix products, arithmetic and copies ran while one was open for 0% -> 0% of each run, Pallas kernels for 0% -> 0%
where the time goes in v1:
time: 58 us; the launch traced here: 57.7 us
  blocking collectives  29.4 us (51%)
  Pallas kernels  23.5 us (41%)
  local copies, waits for them, and re-layouts  4.17 us (7%)
  between operations  0.64 us (1%)
    all_to_all x1, blocking collectives, shards(): recv = lax.all_to_all(packed, 'dp', 0, 0, tiled=True)  29.4 us
    pallas_call x1, Pallas kernels, shards(): pl.pallas_call(functools.partial(hist_kernel, blocks=blocks), out_shape=(...  23.2 us
    unnamed x8, local copies, waits for them, and re-layouts  3.5 us

profile of v1, /device:TPU:1, one launch (start us, length us, event | category | flops | bytes accessed | tf_op | source)
XLA Modules:
  0.0 57.7 jit_solution(11601093340232891226)
XLA Ops:
  0.6 0.7 %pad_bitcast_fusion.node_ref = s32[1,128]{1,0:T(1,128)S(1)} fusion(s32[12]{0:T(128)} %param.9), kind=kLoop, calls=%fused_computation | loop fusion | bytes 560 | tf_op jit(solution)/shard_map/reshape | solution.py:176
  1.3 0.0 copy-start
  1.3 1.4 %copy-done = s32[1536,256]{1,0:T(8,128)S(1)} copy-done((s32[1536,256]{1,0:T(8,128)S(1)}, s32[1536,256]{1,0:T(8,128)}, u32[]{:S(2)}) %copy-start) | copy-done | bytes 1572888
  2.7 0.0 copy-start.1
  2.7 0.7 %copy-done.1 = f32[1536]{0:T(1024)S(1)} copy-done((f32[1536]{0:T(1024)S(1)}, f32[1536]{0:T(1024)}, u32[]{:S(2)}) %copy-start.1) | copy-done | bytes 6168
  3.4 0.0 copy-start.2
  3.4 0.7 %copy-done.2 = s32[1536]{0:T(1024)S(1)} copy-done((s32[1536]{0:T(1024)S(1)}, s32[1536]{0:T(1024)}, u32[]{:S(2)}) %copy-start.2) | copy-done | bytes 6168
  4.1 0.0 copy-start.3
  4.1 0.7 %copy-done.3 = s32[1536]{0:T(1024)S(1)} copy-done((s32[1536]{0:T(1024)S(1)}, s32[1536]{0:T(1024)}, u32[]{:S(2)}) %copy-start.3) | copy-done | bytes 6168
  4.8 0.3 pack.1
  5.1 29.4 %all_to_all.5.recv_ref = s32[32,80,128]{2,1,0:T(8,128)S(1)} all-to-all(s32[32,80,128]{2,1,0:T(8,128)S(1)} %pack.1), channel_id=1, replica_groups=mesh['leaf'=4,'dp'=32] {'dp'}, dimensions={0} | all-to-all | bytes 2621440 | tf_op jit(solution)/shard_map/all_to_all | solution.py:189
  34.5 23.2 %hist.1 = (f32[8,16,256]{2,1,0:T(8,128)}, f32[8,16,256]{2,1,0:T(8,128)}) custom-call(s32[32,12]{1,0:T(8,128)S(1)} %bitcast.6, s32[32,80,128]{2,1,0:T(8,128)S(1)} %all_to_all.5.recv_ref), custom_call_target="tpu_custom_call" | custom-call | tf_op jit(solution)/shard_map/hist/pallas_call | solution.py:193
  (1 shorter events, 0.0 us)
Async XLA Ops:
  1.3 1.4 %copy-start = (s32[1536,256]{1,0:T(8,128)S(1)}, s32[1536,256]{1,0:T(8,128)}, u32[]{:S(2)}) copy-start(s32[1536,256]{1,0:T(8,128)} %bins_ref.1) | copy-start | bytes 4718596
  2.7 0.7 %copy-start.1 = (f32[1536]{0:T(1024)S(1)}, f32[1536]{0:T(1024)}, u32[]{:S(2)}) copy-start(f32[1536]{0:T(1024)} %param.6) | copy-start | bytes 18436
  3.4 0.7 %copy-start.2 = (s32[1536]{0:T(1024)S(1)}, s32[1536]{0:T(1024)}, u32[]{:S(2)}) copy-start(s32[1536]{0:T(1024)} %param.7) | copy-start | bytes 18436
  4.1 0.7 %copy-start.3 = (s32[1536]{0:T(1024)S(1)}, s32[1536]{0:T(1024)}, u32[]{:S(2)}) copy-start(s32[1536]{0:T(1024)} %param.8) | copy-start | bytes 18436

commit v2 on v1

--- a/solution.py
+++ b/solution.py
@@ -51,7 +51,7 @@
     return high, mid, low
 
 
-def hist_kernel(node_smem, recv_ref, sum_ref, cnt_ref, rho_ref, bag_ref, acc_ref, *, blocks):
+def hist_kernel(node_smem, recv_ref, sum_ref, cnt_ref, rho_ref, bag_ref, acc_ref, extra_smem, *, blocks):
     sources = recv_ref.shape[0]
     half = blocks // 2
     base = 8 * half
@@ -116,24 +116,33 @@
     zero_lo = jnp.zeros((32, LANES), BF16)
     zero_hi = jnp.zeros((16, LANES), BF16)
 
-    def one_source(s, carry):
-        for k in range(blocks):
-            tile = recv_ref[s, pl.ds(8 * (k % half), 8), :]
-            if k < half:
-                tile = jnp.bitwise_and(tile, 0xFFFF)
+    group = 4 if blocks % 4 == 0 else 1
+
+    def add_group(s, start, target):
+        lefts, rights = ([], []), ([], [])
+        for n in range(group):
+            k = start + n
+            if isinstance(k, int):
+                tile = recv_ref[s, pl.ds(8 * (k % half), 8), :]
+                if k < half:
+                    tile = jnp.bitwise_and(tile, 0xFFFF)
+                else:
+                    tile = lax.shift_right_logical(tile, 16)
             else:
-                tile = lax.shift_right_logical(tile, 16)
+                upper = (k >= half).astype(I32)
+                tile = recv_ref[s, pl.ds(pl.multiple_of(8 * (k - half * upper), 8), 8), :]
+                tile = jnp.bitwise_and(lax.shift_right_logical(tile, jnp.full(tile.shape, 16 * upper)), 0xFFFF)
             hi = lax.shift_right_logical(tile, 5)
             lo = jnp.bitwise_and(tile, 31)
             row = s * SLOTS + k
+            keep = (node_smem[s, k] == target).astype(F32)
             vals = jnp.concatenate(
                 [
-                    jnp.broadcast_to(rho_ref[pl.ds(row, 1), :], (8, LANES)),
-                    jnp.broadcast_to(bag_ref[pl.ds(row, 1), :], (8, LANES)),
+                    jnp.broadcast_to(rho_ref[pl.ds(row, 1), :] * keep, (8, LANES)),
+                    jnp.broadcast_to(bag_ref[pl.ds(row, 1), :] * keep, (8, LANES)),
                 ],
                 axis=0,
             ).astype(BF16)
-            node = node_smem[s, k]
             for q in range(2):
                 left, right = [], []
                 for f in range(4 * q, 4 * q + 4):
@@ -141,19 +150,38 @@
                     lo_f = jnp.broadcast_to(lo[f : f + 1], (32, LANES)).astype(I16)
                     left.append(jnp.where(hi_f == iota_hi, vals, zero_hi))
                     right.append(jnp.where(lo_f == iota_lo, one, zero_lo))
-                prod = lax.dot_general(
-                    jnp.concatenate(left, axis=0),
-                    jnp.concatenate(right, axis=0),
-                    (((1,), (1,)), ((), ())),
-                    preferred_element_type=F32,
-                )
-                merged = prod[0:16]
-                for i in range(1, 4):
-                    merged = jnp.where(lane_group == i, prod[16 * i : 16 * i + 16], merged)
-                acc_ref[node, pl.ds(16 * q, 16), :] += merged
+                lefts[q].append(jnp.concatenate(left, axis=0))
+                rights[q].append(jnp.concatenate(right, axis=0))
+        for q in range(2):
+            prod = lax.dot_general(
+                jnp.concatenate(lefts[q], axis=1),
+                jnp.concatenate(rights[q], axis=1),
+                (((1,), (1,)), ((), ())),
+                preferred_element_type=F32,
+            )
+            merged = prod[0:16]
+            for i in range(1, 4):
+                merged = jnp.where(lane_group == i, prod[16 * i : 16 * i + 16], merged)
+            acc_ref[target, pl.ds(16 * q, 16), :] += merged
+
+    def one_source(s, found):
+        for start in range(0, blocks, group):
+            add_group(s, start, node_smem[s, start])
+            for k in range(start + 1, start + group):
+                extra_smem[found] = (s * blocks + start) * NODES + node_smem[s, k]
+                found = found + (node_smem[s, k] != node_smem[s, k - 1]).astype(I32)
+        return found
+
+    found = lax.fori_loop(0, sources, one_source, jnp.int32(0), unroll=4)
+
+    def one_extra(e, carry):
+        code = extra_smem[e]
+        place = lax.shift_right_logical(code, 4)
+        s = lax.div(place, blocks)
+        add_group(s, lax.rem(place, blocks), jnp.bitwise_and(code, NODES - 1))
         return carry
 
-    lax.fori_loop(0, sources, one_source, 0)
+    lax.fori_loop(0, found, one_extra, 0)
 
     for v, out_ref in enumerate((sum_ref, cnt_ref)):
         for q in range(2):
@@ -199,6 +227,7 @@
             pltpu.VMEM((dests * SLOTS, LANES), F32),
             pltpu.VMEM((dests * SLOTS, LANES), F32),
             pltpu.VMEM((NODES, 32, LANES), F32),
+            pltpu.SMEM((dests * blocks,), I32),
         ],
         compiler_params=pltpu.CompilerParams(vmem_limit_bytes=32 * 2**20),
         name="hist",

time: 58 us -> 49.3 us (0.85)
  Pallas kernels: 23.5 us -> 14.5 us
    pallas_call x1, Pallas kernels: 23.2 us -> 14.3 us  [shards(): pl.pallas_call(functools.partial(hist_kernel, blocks=blocks), out_shape=(...]
where the time goes in v2:
time: 49.3 us; the launch traced here: 48.8 us
  blocking collectives  29.4 us (60%)
  Pallas kernels  14.5 us (29%)
  local copies, waits for them, and re-layouts  4.17 us (8%)
  between operations  0.64 us (1%)
    all_to_all x1, blocking collectives, shards(): recv = lax.all_to_all(packed, 'dp', 0, 0, tiled=True)  29.4 us
    pallas_call x1, Pallas kernels, shards(): pl.pallas_call(functools.partial(hist_kernel, blocks=blocks), out_shape=(...  14.3 us
    unnamed x8, local copies, waits for them, and re-layouts  3.5 us

profile of v2, /device:TPU:1, one launch (start us, length us, event | category | flops | bytes accessed | tf_op | source)
XLA Modules:
  0.0 48.8 jit_solution(9821069389799455579)
XLA Ops:
  0.6 0.7 %pad_bitcast_fusion.node_ref = s32[1,128]{1,0:T(1,128)S(1)} fusion(s32[12]{0:T(128)} %param.9), kind=kLoop, calls=%fused_computation | loop fusion | bytes 560 | tf_op jit(solution)/shard_map/reshape | solution.py:204
  1.3 0.0 copy-start
  1.3 1.4 %copy-done = s32[1536,256]{1,0:T(8,128)S(1)} copy-done((s32[1536,256]{1,0:T(8,128)S(1)}, s32[1536,256]{1,0:T(8,128)}, u32[]{:S(2)}) %copy-start) | copy-done | bytes 1572888
  2.7 0.0 copy-start.1
  2.7 0.7 %copy-done.1 = f32[1536]{0:T(1024)S(1)} copy-done((f32[1536]{0:T(1024)S(1)}, f32[1536]{0:T(1024)}, u32[]{:S(2)}) %copy-start.1) | copy-done | bytes 6168
  3.4 0.0 copy-start.2
  3.4 0.7 %copy-done.2 = s32[1536]{0:T(1024)S(1)} copy-done((s32[1536]{0:T(1024)S(1)}, s32[1536]{0:T(1024)}, u32[]{:S(2)}) %copy-start.2) | copy-done | bytes 6168
  4.1 0.0 copy-start.3
  4.1 0.7 %copy-done.3 = s32[1536]{0:T(1024)S(1)} copy-done((s32[1536]{0:T(1024)S(1)}, s32[1536]{0:T(1024)}, u32[]{:S(2)}) %copy-start.3) | copy-done | bytes 6168
  4.8 0.3 pack.1
  5.1 29.4 %all_to_all.5.recv_ref = s32[32,80,128]{2,1,0:T(8,128)S(1)} all-to-all(s32[32,80,128]{2,1,0:T(8,128)S(1)} %pack.1), channel_id=1, replica_groups=mesh['leaf'=4,'dp'=32] {'dp'}, dimensions={0} | all-to-all | bytes 2621440 | tf_op jit(solution)/shard_map/all_to_all | solution.py:217
  34.5 14.3 %hist.1 = (f32[8,16,256]{2,1,0:T(8,128)}, f32[8,16,256]{2,1,0:T(8,128)}) custom-call(s32[32,12]{1,0:T(8,128)S(1)} %bitcast.6, s32[32,80,128]{2,1,0:T(8,128)S(1)} %all_to_all.5.recv_ref), custom_call_target="tpu_custom_call" | custom-call | tf_op jit(solution)/shard_map/hist/pallas_call | solution.py:221
  (1 shorter events, 0.0 us)
Async XLA Ops:
  1.3 1.4 %copy-start = (s32[1536,256]{1,0:T(8,128)S(1)}, s32[1536,256]{1,0:T(8,128)}, u32[]{:S(2)}) copy-start(s32[1536,256]{1,0:T(8,128)} %bins_ref.1) | copy-start | bytes 4718596
  2.7 0.7 %copy-start.1 = (f32[1536]{0:T(1024)S(1)}, f32[1536]{0:T(1024)}, u32[]{:S(2)}) copy-start(f32[1536]{0:T(1024)} %param.6) | copy-start | bytes 18436
  3.4 0.7 %copy-start.2 = (s32[1536]{0:T(1024)S(1)}, s32[1536]{0:T(1024)}, u32[]{:S(2)}) copy-start(s32[1536]{0:T(1024)} %param.7) | copy-start | bytes 18436
  4.1 0.7 %copy-start.3 = (s32[1536]{0:T(1024)S(1)}, s32[1536]{0:T(1024)}, u32[]{:S(2)}) copy-start(s32[1536]{0:T(1024)} %param.8) | copy-start | bytes 18436

commit v3 on v2

--- a/solution.py
+++ b/solution.py
@@ -18,29 +18,52 @@
 Y_SCALE = float(2**28)
 
 
-def pack_kernel(bins_ref, y_ref, w_ref, b_ref, node_ref, out_ref):
+def pack_kernel(
+    bins_hbm, y_hbm, w_hbm, b_hbm, node_hbm, out_ref, bins_ref, y_ref, w_ref, b_ref, node_smem, sems
+):
+    copies = [
+        pltpu.make_async_copy(src, dst, sems.at[n])
+        for n, (src, dst) in enumerate(
+            (
+                (bins_hbm, bins_ref),
+                (y_hbm, y_ref),
+                (w_hbm, w_ref),
+                (b_hbm, b_ref),
+                (node_hbm, node_smem),
+            )
+        )
+    ]
+    for copy in copies:
+        copy.start()
     dests = out_ref.shape[0]
     blocks = y_ref.shape[0]
     half = blocks // 2
+    base = 8 * half
+    for copy in copies[1:]:
+        copy.wait()
+    fixed = jnp.round(y_ref[...] * Y_SCALE).astype(I32)
+    flags = jnp.bitwise_or(w_ref[...], lax.shift_left(b_ref[...], 16))
+    lane = lax.broadcasted_iota(I32, (1, LANES), 1)
+    nodes = jnp.zeros((1, LANES), I32)
+    for k in range(blocks):
+        nodes = jnp.where(lane == k, node_smem[k], nodes)
+    tail = jnp.concatenate(
+        [
+            fixed,
+            nodes,
+            jnp.zeros((SLOTS - blocks - 1, LANES), I32),
+            flags,
+            jnp.zeros((SLOTS - blocks, LANES), I32),
+        ],
+        axis=0,
+    )
+    out_ref[:, pl.ds(base, 2 * SLOTS), :] = jnp.broadcast_to(tail[None], (dests,) + tail.shape)
+    copies[0].wait()
     for t in range(half):
         low = bins_ref[pl.ds(LANES * t, LANES), :]
         high = bins_ref[pl.ds(LANES * (t + half), LANES), :]
         packed = jnp.bitwise_or(low, lax.shift_left(high, 16)).T
         out_ref[:, pl.ds(8 * t, 8), :] = packed.reshape(dests, 8, LANES)
-    base = 8 * half
-    fixed = jnp.round(y_ref[...] * Y_SCALE).astype(I32)
-    flags = jnp.bitwise_or(w_ref[...], lax.shift_left(b_ref[...], 16))
-    tail = jnp.concatenate(
-        [
-            fixed,
-            node_ref[...],
-            jnp.zeros((SLOTS - blocks - 1, LANES), I32),
-            flags,
-            jnp.zeros((SLOTS - blocks, LANES), I32),
-        ],
-        axis=0,
-    )
-    out_ref[:, pl.ds(base, 2 * SLOTS), :] = jnp.broadcast_to(tail[None], (dests,) + tail.shape)
 
 
 def split3(x):
@@ -109,17 +132,15 @@
     bag_ref[...] = b
 
     acc_ref[...] = jnp.zeros_like(acc_ref)
-    iota_hi = jnp.bitwise_and(lax.broadcasted_iota(I32, (16, LANES), 0), 7).astype(I16)
-    iota_lo = lax.broadcasted_iota(I32, (32, LANES), 0).astype(I16)
-    lane_group = lax.shift_right_logical(lax.broadcasted_iota(I32, (16, LANES), 1), 5)
-    one = jnp.ones((32, LANES), BF16)
-    zero_lo = jnp.zeros((32, LANES), BF16)
-    zero_hi = jnp.zeros((16, LANES), BF16)
-
+    iota_bin = lax.broadcasted_iota(I32, (16, LANES), 0).astype(I16)
+    lane_group = lax.shift_right_logical(lax.broadcasted_iota(I32, (NODES, LANES), 1), 4)
+    merge_group = lax.shift_right_logical(lax.broadcasted_iota(I32, (32, LANES), 1), 4)
+    one = jnp.ones((16, LANES), BF16)
+    zero = jnp.zeros((16, LANES), BF16)
     group = 4 if blocks % 4 == 0 else 1
 
     def add_group(s, start, target):
-        lefts, rights = ([], []), ([], [])
+        lefts, rights = [], []
         for n in range(group):
             k = start + n
             if isinstance(k, int):
@@ -132,68 +153,64 @@
                 upper = (k >= half).astype(I32)
                 tile = recv_ref[s, pl.ds(pl.multiple_of(8 * (k - half * upper), 8), 8), :]
                 tile = jnp.bitwise_and(lax.shift_right_logical(tile, jnp.full(tile.shape, 16 * upper)), 0xFFFF)
-            hi = lax.shift_right_logical(tile, 5)
-            lo = jnp.bitwise_and(tile, 31)
+            hi = lax.shift_right_logical(tile, 4)
+            lo = jnp.bitwise_and(tile, 15)
             row = s * SLOTS + k
             keep = (node_smem[s, k] == target).astype(F32)
-            vals = jnp.concatenate(
-                [
-                    jnp.broadcast_to(rho_ref[pl.ds(row, 1), :] * keep, (8, LANES)),
-                    jnp.broadcast_to(bag_ref[pl.ds(row, 1), :] * keep, (8, LANES)),
-                ],
-                axis=0,
-            ).astype(BF16)
-            for q in range(2):
-                left, right = [], []
-                for f in range(4 * q, 4 * q + 4):
-                    hi_f = jnp.broadcast_to(hi[f : f + 1], (16, LANES)).astype(I16)
-                    lo_f = jnp.broadcast_to(lo[f : f + 1], (32, LANES)).astype(I16)
-                    left.append(jnp.where(hi_f == iota_hi, vals, zero_hi))
-                    right.append(jnp.where(lo_f == iota_lo, one, zero_lo))
-                lefts[q].append(jnp.concatenate(left, axis=0))
-                rights[q].append(jnp.concatenate(right, axis=0))
-        for q in range(2):
-            prod = lax.dot_general(
-                jnp.concatenate(lefts[q], axis=1),
-                jnp.concatenate(rights[q], axis=1),
-                (((1,), (1,)), ((), ())),
-                preferred_element_type=F32,
-            )
-            merged = prod[0:16]
-            for i in range(1, 4):
-                merged = jnp.where(lane_group == i, prod[16 * i : 16 * i + 16], merged)
-            acc_ref[target, pl.ds(16 * q, 16), :] += merged
+            rho = jnp.broadcast_to(rho_ref[pl.ds(row, 1), :] * keep, (16, LANES)).astype(BF16)
+            bag = jnp.broadcast_to(bag_ref[pl.ds(row, 1), :] * keep, (16, LANES)).astype(BF16)
+            left, right = [], []
+            for f in range(8):
+                hot = jnp.broadcast_to(hi[f : f + 1], (16, LANES)).astype(I16) == iota_bin
+                left += [jnp.where(hot, rho, zero), jnp.where(hot, bag, zero)]
+                hot = jnp.broadcast_to(lo[f : f + 1], (16, LANES)).astype(I16) == iota_bin
+                right.append(jnp.where(hot, one, zero))
+            lefts.append(jnp.concatenate(left, axis=0))
+            rights.append(jnp.concatenate(right, axis=0))
+        prod = lax.dot_general(
+            jnp.concatenate(lefts, axis=1),
+            jnp.concatenate(rights, axis=1),
+            (((1,), (1,)), ((), ())),
+            preferred_element_type=F32,
+        )
+        merged = prod[0:32]
+        for f in range(1, 8):
+            merged = jnp.where(merge_group == f, prod[32 * f : 32 * f + 32], merged)
+        return merged
 
     def one_source(s, found):
+        pending = []
         for start in range(0, blocks, group):
-            add_group(s, start, node_smem[s, start])
+            pending.append((node_smem[s, start], add_group(s, start, node_smem[s, start])))
             for k in range(start + 1, start + group):
                 extra_smem[found] = (s * blocks + start) * NODES + node_smem[s, k]
                 found = found + (node_smem[s, k] != node_smem[s, k - 1]).astype(I32)
+        for target, merged in pending:
+            acc_ref[target] += merged
         return found
 
-    found = lax.fori_loop(0, sources, one_source, jnp.int32(0), unroll=4)
+    found = lax.fori_loop(0, sources, one_source, jnp.int32(0), unroll=8)
 
     def one_extra(e, carry):
         code = extra_smem[e]
         place = lax.shift_right_logical(code, 4)
         s = lax.div(place, blocks)
-        add_group(s, lax.rem(place, blocks), jnp.bitwise_and(code, NODES - 1))
+        target = jnp.bitwise_and(code, NODES - 1)
+        acc_ref[target] += add_group(s, lax.rem(place, blocks), target)
         return carry
 
     lax.fori_loop(0, found, one_extra, 0)
 
     for v, out_ref in enumerate((sum_ref, cnt_ref)):
-        for q in range(2):
-            for c in range(2):
-                pieces = [acc_ref[:, 16 * q + 8 * v + 4 * c + g, :] for g in range(4)]
-                for i in range(4):
-                    out = None
-                    for g in range(4):
-                        shift = (32 * (g - i)) % LANES
-                        moved = pltpu.roll(pieces[g], shift, 1) if shift else pieces[g]
-                        out = moved if out is None else jnp.where(lane_group == g, moved, out)
-                    out_ref[4 * q + i, :, pl.ds(LANES * c, LANES)] = out
+        for c in range(2):
+            pieces = [acc_ref[:, 16 * v + 8 * c + g, :] for g in range(8)]
+            for f in range(8):
+                out = None
+                for g in range(8):
+                    shift = (16 * (g - f)) % LANES
+                    moved = pltpu.roll(pieces[g], shift, 1) if shift else pieces[g]
+                    out = moved if out is None else jnp.where(lane_group == g, moved, out)
+                out_ref[f, :, pl.ds(LANES * c, LANES)] = out
 
 
 def shards(bins, outcome, treatment, bag, block_node):
@@ -201,18 +218,27 @@
     dests = lax.axis_size("dp")
     own = bins.shape[1] // dests
     height = 8 * (blocks // 2) + 2 * SLOTS
-    node_row = jnp.pad(block_node, (0, LANES - blocks)).reshape(1, LANES)
     packed = pl.pallas_call(
         pack_kernel,
         out_shape=jax.ShapeDtypeStruct((dests, height, LANES), I32),
-        compiler_params=pltpu.CompilerParams(vmem_limit_bytes=32 * 2**20),
+        in_specs=[pl.BlockSpec(memory_space=pl.ANY)] * 5,
+        out_specs=pl.BlockSpec(memory_space=pltpu.VMEM),
+        scratch_shapes=[
+            pltpu.VMEM(bins.shape, I32),
+            pltpu.VMEM((blocks, LANES), F32),
+            pltpu.VMEM((blocks, LANES), I32),
+            pltpu.VMEM((blocks, LANES), I32),
+            pltpu.SMEM((blocks,), I32),
+            pltpu.SemaphoreType.DMA((5,)),
+        ],
+        compiler_params=pltpu.CompilerParams(vmem_limit_bytes=60 * 2**20),
         name="pack",
     )(
         bins,
         outcome.reshape(blocks, LANES),
         treatment.reshape(blocks, LANES),
         bag.reshape(blocks, LANES),
-        node_row,
+        block_node,
     )
     recv = lax.all_to_all(packed, "dp", 0, 0, tiled=True)
     nodes = recv[:, 8 * (blocks // 2) + blocks, :blocks]

time: 49.3 us -> 46.4 us (0.941)
  local copies, waits for them, and re-layouts: 4.17 us -> 0.02 us
  Pallas kernels: 14.5 us -> 15.9 us
    unnamed x8 -> x0, local copies, waits for them, and re-layouts: 3.5 us -> none
    pallas_call x1, Pallas kernels: 0.27 us -> 2.79 us  [shards(): pl.pallas_call(pack_kernel, out_shape=jax.ShapeDtypeStruct((dests, height...]
    pallas_call x1, Pallas kernels: 14.3 us -> 13.1 us  [shards(): pl.pallas_call(functools.partial(hist_kernel, blocks=blocks), out_shape=(...]
    reshape x1 -> x0, local copies, waits for them, and re-layouts: 0.66 us -> none  [shards(): node_row = jnp.pad(block_node, (0, LANES - blocks)).reshape(1, LANES)]
where the time goes in v3:
time: 46.4 us; the launch traced here: 46.2 us
  blocking collectives  29.6 us (64%)
  Pallas kernels  15.9 us (34%)
  between operations  0.64 us (1%)
    all_to_all x1, blocking collectives, shards(): recv = lax.all_to_all(packed, 'dp', 0, 0, tiled=True)  29.6 us
    pallas_call x1, Pallas kernels, shards(): pl.pallas_call(functools.partial(hist_kernel, blocks=blocks), out_shape=(...  13.1 us
    pallas_call x1, Pallas kernels, shards(): pl.pallas_call(pack_kernel, out_shape=jax.ShapeDtypeStruct((dests, height...  2.79 us

profile of v3, /device:TPU:1, one launch (start us, length us, event | category | flops | bytes accessed | tf_op | source)
XLA Modules:
  0.0 46.2 jit_solution(6637206654050937700)
XLA Ops:
  0.6 2.8 %pack.1 = s32[32,80,128]{2,1,0:T(8,128)} custom-call(s32[1536,256]{1,0:T(8,128)} %bins_hbm.1, f32[12,128]{1,0:T(8,128)} %bitcast.5, s32[12,128]{1,0:T(8,128)} %bitcast.6, s32[12,128]{1,0:T(8,128)} %bitcast.7, s32[12]{0:T(128)} %node_hbm.1), custom_call_target="tpu_custom_call" | custom-call | tf_op jit(solution)/shard_map/pack/pallas_call | solution.py:221
  3.4 29.6 %all_to_all.5.recv_ref = s32[32,80,128]{2,1,0:T(8,128)S(1)} all-to-all(s32[32,80,128]{2,1,0:T(8,128)} %pack.1), channel_id=1, replica_groups=mesh['leaf'=4,'dp'=32] {'dp'}, dimensions={0} | all-to-all | bytes 2621440 | tf_op jit(solution)/shard_map/all_to_all | solution.py:243
  33.1 13.1 %hist.1 = (f32[8,16,256]{2,1,0:T(8,128)}, f32[8,16,256]{2,1,0:T(8,128)}) custom-call(s32[32,12]{1,0:T(8,128)S(1)} %bitcast.4, s32[32,80,128]{2,1,0:T(8,128)S(1)} %all_to_all.5.recv_ref), custom_call_target="tpu_custom_call" | custom-call | tf_op jit(solution)/shard_map/hist/pallas_call | solution.py:247
  (1 shorter events, 0.0 us)

commit v4 on v3

--- a/solution.py
+++ b/solution.py
@@ -139,7 +139,7 @@
     zero = jnp.zeros((16, LANES), BF16)
     group = 4 if blocks % 4 == 0 else 1
 
-    def add_group(s, start, target):
+    def group_sums(s, start, target):
         lefts, rights = [], []
         for n in range(group):
             k = start + n
@@ -181,29 +181,37 @@
     def one_source(s, found):
         pending = []
         for start in range(0, blocks, group):
-            pending.append((node_smem[s, start], add_group(s, start, node_smem[s, start])))
+            pending.append((node_smem[s, start], group_sums(s, start, node_smem[s, start])))
             for k in range(start + 1, start + group):
-                extra_smem[found] = (s * blocks + start) * NODES + node_smem[s, k]
+                extra_smem[found] = (s * blocks + start) * 32 + node_smem[s, k]
                 found = found + (node_smem[s, k] != node_smem[s, k - 1]).astype(I32)
         for target, merged in pending:
             acc_ref[target] += merged
         return found
 
-    found = lax.fori_loop(0, sources, one_source, jnp.int32(0), unroll=8)
-
-    def one_extra(e, carry):
-        code = extra_smem[e]
-        place = lax.shift_right_logical(code, 4)
-        s = lax.div(place, blocks)
-        target = jnp.bitwise_and(code, NODES - 1)
-        acc_ref[target] += add_group(s, lax.rem(place, blocks), target)
+    found = lax.fori_loop(0, sources, one_source, jnp.int32(0), unroll=16)
+
+    batch = 4
+    for n in range(batch - 1):
+        extra_smem[found + n] = jnp.int32(NODES)
+
+    def some_extras(e, carry):
+        pending = []
+        for n in range(batch):
+            code = extra_smem[batch * e + n]
+            target = jnp.bitwise_and(code, 31)
+            place = lax.shift_right_logical(code, 5)
+            start = lax.rem(place, blocks)
+            pending.append((target, group_sums(lax.div(place, blocks), start, target)))
+        for target, merged in pending:
+            acc_ref[target] += merged
         return carry
 
-    lax.fori_loop(0, found, one_extra, 0)
+    lax.fori_loop(0, lax.div(found + batch - 1, batch), some_extras, 0)
 
     for v, out_ref in enumerate((sum_ref, cnt_ref)):
         for c in range(2):
-            pieces = [acc_ref[:, 16 * v + 8 * c + g, :] for g in range(8)]
+            pieces = [acc_ref[:NODES, 16 * v + 8 * c + g, :] for g in range(8)]
             for f in range(8):
                 out = None
                 for g in range(8):
@@ -252,7 +260,7 @@
         scratch_shapes=[
             pltpu.VMEM((dests * SLOTS, LANES), F32),
             pltpu.VMEM((dests * SLOTS, LANES), F32),
-            pltpu.VMEM((NODES, 32, LANES), F32),
+            pltpu.VMEM((NODES + 1, 32, LANES), F32),
             pltpu.SMEM((dests * blocks,), I32),
         ],
         compiler_params=pltpu.CompilerParams(vmem_limit_bytes=32 * 2**20),

time: 46.4 us -> 44.7 us (0.963)
  Pallas kernels: 15.9 us -> 13.9 us
    pallas_call x1, Pallas kernels: 13.1 us -> 11.1 us  [shards(): pl.pallas_call(functools.partial(hist_kernel, blocks=blocks), out_shape=(...]
where the time goes in v4:
time: 44.7 us; the launch traced here: 44.2 us
  blocking collectives  29.6 us (66%)
  Pallas kernels  13.9 us (31%)
  between operations  0.64 us (1%)
    all_to_all x1, blocking collectives, shards(): recv = lax.all_to_all(packed, 'dp', 0, 0, tiled=True)  29.6 us
    pallas_call x1, Pallas kernels, shards(): pl.pallas_call(functools.partial(hist_kernel, blocks=blocks), out_shape=(...  11.1 us
    pallas_call x1, Pallas kernels, shards(): pl.pallas_call(pack_kernel, out_shape=jax.ShapeDtypeStruct((dests, height...  2.79 us

profile of v4, /device:TPU:1, one launch (start us, length us, event | category | flops | bytes accessed | tf_op | source)
XLA Modules:
  0.0 44.2 jit_solution(13654935725277695022)
XLA Ops:
  0.6 2.8 %pack.1 = s32[32,80,128]{2,1,0:T(8,128)} custom-call(s32[1536,256]{1,0:T(8,128)} %bins_hbm.1, f32[12,128]{1,0:T(8,128)} %bitcast.5, s32[12,128]{1,0:T(8,128)} %bitcast.6, s32[12,128]{1,0:T(8,128)} %bitcast.7, s32[12]{0:T(128)} %node_hbm.1), custom_call_target="tpu_custom_call" | custom-call | tf_op jit(solution)/shard_map/pack/pallas_call | solution.py:229
  3.4 29.6 %all_to_all.5.recv_ref = s32[32,80,128]{2,1,0:T(8,128)S(1)} all-to-all(s32[32,80,128]{2,1,0:T(8,128)} %pack.1), channel_id=1, replica_groups=mesh['leaf'=4,'dp'=32] {'dp'}, dimensions={0} | all-to-all | bytes 2621440 | tf_op jit(solution)/shard_map/all_to_all | solution.py:251
  33.1 11.1 %hist.1 = (f32[8,16,256]{2,1,0:T(8,128)}, f32[8,16,256]{2,1,0:T(8,128)}) custom-call(s32[32,12]{1,0:T(8,128)S(1)} %bitcast.4, s32[32,80,128]{2,1,0:T(8,128)S(1)} %all_to_all.5.recv_ref), custom_call_target="tpu_custom_call" | custom-call | tf_op jit(solution)/shard_map/hist/pallas_call | solution.py:255
  (1 shorter events, 0.0 us)

commit v5 on v4

--- a/solution.py
+++ b/solution.py
@@ -15,7 +15,8 @@
 BF16 = jnp.bfloat16
 I32 = jnp.int32
 I16 = jnp.int16
-Y_SCALE = float(2**28)
+Y_SCALE = float(2**20)
+TAIL = 24
 
 
 def pack_kernel(
@@ -41,23 +42,27 @@
     base = 8 * half
     for copy in copies[1:]:
         copy.wait()
-    fixed = jnp.round(y_ref[...] * Y_SCALE).astype(I32)
+    fixed = jnp.bitwise_and(jnp.round(y_ref[...] * Y_SCALE).astype(I32), 0xFFFFFF)
     flags = jnp.bitwise_or(w_ref[...], lax.shift_left(b_ref[...], 16))
     lane = lax.broadcasted_iota(I32, (1, LANES), 1)
     nodes = jnp.zeros((1, LANES), I32)
     for k in range(blocks):
         nodes = jnp.where(lane == k, node_smem[k], nodes)
+    last = fixed[11:12]
+    top = lax.shift_left(lax.shift_right_logical(last, 16), 24)
     tail = jnp.concatenate(
         [
-            fixed,
-            nodes,
-            jnp.zeros((SLOTS - blocks - 1, LANES), I32),
-            flags,
-            jnp.zeros((SLOTS - blocks, LANES), I32),
+            fixed[0:3],
+            jnp.bitwise_or(fixed[3:4], top),
+            fixed[4:8],
+            flags[8:12],
+            fixed[8:11],
+            jnp.bitwise_or(jnp.bitwise_and(last, 0xFFFF), lax.shift_left(nodes, 16)),
+            flags[0:8],
         ],
         axis=0,
     )
-    out_ref[:, pl.ds(base, 2 * SLOTS), :] = jnp.broadcast_to(tail[None], (dests,) + tail.shape)
+    out_ref[:, pl.ds(base, TAIL), :] = jnp.broadcast_to(tail[None], (dests,) + tail.shape)
     copies[0].wait()
     for t in range(half):
         low = bins_ref[pl.ds(LANES * t, LANES), :]
@@ -80,14 +85,23 @@
     base = 8 * half
     rows = sources * SLOTS
 
-    first = recv_ref[:, pl.ds(base, SLOTS), :]
-    flags = recv_ref[:, pl.ds(base + SLOTS, SLOTS), :].reshape(rows, LANES)
-    y = first.reshape(rows, LANES).astype(F32) * (1.0 / Y_SCALE)
+    part_a, part_b, part_c = [recv_ref[:, pl.ds(base + 8 * p, 8), :] for p in range(3)]
+    sub8 = lax.broadcasted_iota(I32, part_b.shape, 1)
+    flags = jnp.concatenate([part_c, jnp.where(sub8 < 4, part_b, 0)], axis=1).reshape(rows, LANES)
+    upper = pltpu.roll(part_b, 4, 1)
+    mixed = jnp.bitwise_or(
+        jnp.bitwise_and(upper, 0xFFFF),
+        lax.shift_left(lax.shift_right_logical(part_a, 24), 16),
+    )
+    fixed = jnp.concatenate([part_a, jnp.where(sub8 == 3, mixed, upper)], axis=1)
+    fixed = lax.shift_right_arithmetic(lax.shift_left(fixed, 8), 8)
+    y = fixed.reshape(rows, LANES).astype(F32) * (1.0 / Y_SCALE)
     w = jnp.bitwise_and(flags, 0xFFFF).astype(F32)
     b = lax.shift_right_logical(flags, 16).astype(F32)
     sub = lax.broadcasted_iota(I32, (sources, SLOTS, LANES), 1)
     lane = lax.broadcasted_iota(I32, (sources, SLOTS, LANES), 2)
-    node_row = jnp.broadcast_to(first[:, blocks : blocks + 1, :], first.shape).astype(F32)
+    node_row = lax.shift_right_logical(part_b[:, 7:8, :], 16).astype(F32)
+    node_row = jnp.broadcast_to(node_row, (sources, SLOTS, LANES))
     node_col = jnp.sum(jnp.where(sub == lane, node_row, 0.0), axis=2, keepdims=True)
     node_col = node_col.reshape(rows, 1)
     lanes = lax.broadcasted_iota(I32, (rows, LANES), 1)
@@ -225,7 +239,8 @@
     blocks = block_node.shape[0]
     dests = lax.axis_size("dp")
     own = bins.shape[1] // dests
-    height = 8 * (blocks // 2) + 2 * SLOTS
+    base = 8 * (blocks // 2)
+    height = base + TAIL
     packed = pl.pallas_call(
         pack_kernel,
         out_shape=jax.ShapeDtypeStruct((dests, height, LANES), I32),
@@ -249,7 +264,7 @@
         block_node,
     )
     recv = lax.all_to_all(packed, "dp", 0, 0, tiled=True)
-    nodes = recv[:, 8 * (blocks // 2) + blocks, :blocks]
+    nodes = lax.shift_right_logical(recv[:, base + 15, :blocks], 16)
     out = jax.ShapeDtypeStruct((own, NODES, BINS), F32)
     vmem = pl.BlockSpec(memory_space=pltpu.VMEM)
     return pl.pallas_call(

time: 44.7 us -> 42.9 us (0.960); the launches traced: 44.2 us -> 42.9 us
  blocking collectives: 29.6 us -> 28.3 us
    all_to_all x1, blocking collectives: 29.6 us -> 28.3 us  [shards(): recv = lax.all_to_all(packed, 'dp', 0, 0, tiled=True)]
where the time goes in v5:
time: 42.9 us
  blocking collectives  28.3 us (66%)
  Pallas kernels  13.9 us (32%)
  between operations  0.64 us (1%)
    all_to_all x1, blocking collectives, shards(): recv = lax.all_to_all(packed, 'dp', 0, 0, tiled=True)  28.3 us
    pallas_call x1, Pallas kernels, shards(): pl.pallas_call(functools.partial(hist_kernel, blocks=blocks), out_shape=(...  11.2 us
    pallas_call x1, Pallas kernels, shards(): pl.pallas_call(pack_kernel, out_shape=jax.ShapeDtypeStruct((dests, height...  2.73 us

profile of v5, /device:TPU:1, one launch (start us, length us, event | category | flops | bytes accessed | tf_op | source)
XLA Modules:
  0.0 42.9 jit_solution(285930446731289468)
XLA Ops:
  0.6 2.7 %pack.1 = s32[32,72,128]{2,1,0:T(8,128)} custom-call(s32[1536,256]{1,0:T(8,128)} %bins_hbm.1, f32[12,128]{1,0:T(8,128)} %bitcast.5, s32[12,128]{1,0:T(8,128)} %bitcast.6, s32[12,128]{1,0:T(8,128)} %bitcast.7, s32[12]{0:T(128)} %node_hbm.1), custom_call_target="tpu_custom_call" | custom-call | tf_op jit(solution)/shard_map/pack/pallas_call | solution.py:244
  3.4 28.3 %all_to_all.5.recv_ref = s32[32,72,128]{2,1,0:T(8,128)S(1)} all-to-all(s32[32,72,128]{2,1,0:T(8,128)} %pack.1), channel_id=1, replica_groups=mesh['leaf'=4,'dp'=32] {'dp'}, dimensions={0} | all-to-all | bytes 2359296 | tf_op jit(solution)/shard_map/all_to_all | solution.py:266
  31.7 11.2 %hist.1 = (f32[8,16,256]{2,1,0:T(8,128)}, f32[8,16,256]{2,1,0:T(8,128)}) custom-call(s32[32,12]{1,0:T(8,128)S(1)} %bitcast.4, s32[32,72,128]{2,1,0:T(8,128)S(1)} %all_to_all.5.recv_ref), custom_call_target="tpu_custom_call" | custom-call | tf_op jit(solution)/shard_map/hist/pallas_call | solution.py:270
  (1 shorter events, 0.0 us)

commit v6 on v5

--- a/solution.py
+++ b/solution.py
@@ -205,7 +205,7 @@
 
     found = lax.fori_loop(0, sources, one_source, jnp.int32(0), unroll=16)
 
-    batch = 4
+    batch = 8
     for n in range(batch - 1):
         extra_smem[found + n] = jnp.int32(NODES)
 

time: 42.9 us -> 43.2 us (level)
  no operation moved by 1% of the time
where the time goes in v6:
time: 43.2 us; the launch traced here: 43 us
  blocking collectives  28.3 us (66%)
  Pallas kernels  14 us (32%)
  between operations  0.64 us (1%)
    all_to_all x1, blocking collectives, shards(): recv = lax.all_to_all(packed, 'dp', 0, 0, tiled=True)  28.3 us
    pallas_call x1, Pallas kernels, shards(): pl.pallas_call(functools.partial(hist_kernel, blocks=blocks), out_shape=(...  11.2 us
    pallas_call x1, Pallas kernels, shards(): pl.pallas_call(pack_kernel, out_shape=jax.ShapeDtypeStruct((dests, height...  2.73 us

profile of v6, /device:TPU:1, one launch (start us, length us, event | category | flops | bytes accessed | tf_op | source)
XLA Modules:
  0.0 43.0 jit_solution(14645140853909683317)
XLA Ops:
  0.6 2.7 %pack.1 = s32[32,72,128]{2,1,0:T(8,128)} custom-call(s32[1536,256]{1,0:T(8,128)} %bins_hbm.1, f32[12,128]{1,0:T(8,128)} %bitcast.5, s32[12,128]{1,0:T(8,128)} %bitcast.6, s32[12,128]{1,0:T(8,128)} %bitcast.7, s32[12]{0:T(128)} %node_hbm.1), custom_call_target="tpu_custom_call" | custom-call | tf_op jit(solution)/shard_map/pack/pallas_call | solution.py:244
  3.4 28.3 %all_to_all.5.recv_ref = s32[32,72,128]{2,1,0:T(8,128)S(1)} all-to-all(s32[32,72,128]{2,1,0:T(8,128)} %pack.1), channel_id=1, replica_groups=mesh['leaf'=4,'dp'=32] {'dp'}, dimensions={0} | all-to-all | bytes 2359296 | tf_op jit(solution)/shard_map/all_to_all | solution.py:266
  31.7 11.2 %hist.1 = (f32[8,16,256]{2,1,0:T(8,128)}, f32[8,16,256]{2,1,0:T(8,128)}) custom-call(s32[32,12]{1,0:T(8,128)S(1)} %bitcast.4, s32[32,72,128]{2,1,0:T(8,128)S(1)} %all_to_all.5.recv_ref), custom_call_target="tpu_custom_call" | custom-call | tf_op jit(solution)/shard_map/hist/pallas_call | solution.py:270
  (1 shorter events, 0.0 us)

commit v7 on v6

--- a/solution.py
+++ b/solution.py
@@ -151,9 +151,9 @@
     merge_group = lax.shift_right_logical(lax.broadcasted_iota(I32, (32, LANES), 1), 4)
     one = jnp.ones((16, LANES), BF16)
     zero = jnp.zeros((16, LANES), BF16)
-    group = 4 if blocks % 4 == 0 else 1
-
-    def group_sums(s, start, target):
+    group = 2 if blocks % 2 == 0 else 1
+
+    def group_sums(s, start, target, first_is_target=False):
         lefts, rights = [], []
         for n in range(group):
             k = start + n
@@ -170,9 +170,13 @@
             hi = lax.shift_right_logical(tile, 4)
             lo = jnp.bitwise_and(tile, 15)
             row = s * SLOTS + k
-            keep = (node_smem[s, k] == target).astype(F32)
-            rho = jnp.broadcast_to(rho_ref[pl.ds(row, 1), :] * keep, (16, LANES)).astype(BF16)
-            bag = jnp.broadcast_to(bag_ref[pl.ds(row, 1), :] * keep, (16, LANES)).astype(BF16)
+            rho = rho_ref[pl.ds(row, 1), :]
+            bag = bag_ref[pl.ds(row, 1), :]
+            if n > 0 or not first_is_target:
+                keep = (node_smem[s, k] == target).astype(F32)
+                rho, bag = rho * keep, bag * keep
+            rho = jnp.broadcast_to(rho, (16, LANES)).astype(BF16)
+            bag = jnp.broadcast_to(bag, (16, LANES)).astype(BF16)
             left, right = [], []
             for f in range(8):
                 hot = jnp.broadcast_to(hi[f : f + 1], (16, LANES)).astype(I16) == iota_bin
@@ -195,7 +199,7 @@
     def one_source(s, found):
         pending = []
         for start in range(0, blocks, group):
-            pending.append((node_smem[s, start], group_sums(s, start, node_smem[s, start])))
+            pending.append((node_smem[s, start], group_sums(s, start, node_smem[s, start], True)))
             for k in range(start + 1, start + group):
                 extra_smem[found] = (s * blocks + start) * 32 + node_smem[s, k]
                 found = found + (node_smem[s, k] != node_smem[s, k - 1]).astype(I32)

time: 43.2 us -> 42.4 us (0.981)
  Pallas kernels: 14 us -> 13 us
    pallas_call x1, Pallas kernels: 11.2 us -> 10.2 us  [shards(): pl.pallas_call(functools.partial(hist_kernel, blocks=blocks), out_shape=(...]
where the time goes in v7:
time: 42.4 us; the launch traced here: 41.9 us
  blocking collectives  28.3 us (67%)
  Pallas kernels  13 us (31%)
  between operations  0.64 us (2%)
    all_to_all x1, blocking collectives, shards(): recv = lax.all_to_all(packed, 'dp', 0, 0, tiled=True)  28.3 us
    pallas_call x1, Pallas kernels, shards(): pl.pallas_call(functools.partial(hist_kernel, blocks=blocks), out_shape=(...  10.2 us
    pallas_call x1, Pallas kernels, shards(): pl.pallas_call(pack_kernel, out_shape=jax.ShapeDtypeStruct((dests, height...  2.73 us

profile of v7, /device:TPU:1, one launch (start us, length us, event | category | flops | bytes accessed | tf_op | source)
XLA Modules:
  0.0 41.9 jit_solution(2793144086915439968)
XLA Ops:
  0.6 2.7 %pack.1 = s32[32,72,128]{2,1,0:T(8,128)} custom-call(s32[1536,256]{1,0:T(8,128)} %bins_hbm.1, f32[12,128]{1,0:T(8,128)} %bitcast.5, s32[12,128]{1,0:T(8,128)} %bitcast.6, s32[12,128]{1,0:T(8,128)} %bitcast.7, s32[12]{0:T(128)} %node_hbm.1), custom_call_target="tpu_custom_call" | custom-call | tf_op jit(solution)/shard_map/pack/pallas_call | solution.py:248
  3.4 28.3 %all_to_all.5.recv_ref = s32[32,72,128]{2,1,0:T(8,128)S(1)} all-to-all(s32[32,72,128]{2,1,0:T(8,128)} %pack.1), channel_id=1, replica_groups=mesh['leaf'=4,'dp'=32] {'dp'}, dimensions={0} | all-to-all | bytes 2359296 | tf_op jit(solution)/shard_map/all_to_all | solution.py:270
  31.7 10.2 %hist.1 = (f32[8,16,256]{2,1,0:T(8,128)}, f32[8,16,256]{2,1,0:T(8,128)}) custom-call(s32[32,12]{1,0:T(8,128)S(1)} %bitcast.4, s32[32,72,128]{2,1,0:T(8,128)S(1)} %all_to_all.5.recv_ref), custom_call_target="tpu_custom_call" | custom-call | tf_op jit(solution)/shard_map/hist/pallas_call | solution.py:274
  (1 shorter events, 0.0 us)
